TPU v7x, 512 devices: a whole 4x4x16 slice. The times are simulated.
512 devices in a mesh: cols: 128 (over z, y, core), rep: 4 (over x).
Axes of the slice: x: 4, y: 4, z: 16, core: 2. Of those that a mesh axis runs over, the one named last changes fastest.
Arguments:
- taxa_states: int32 [32, 65536], P(None, ('cols', 'rep')), may hold values from 0 to 19
- outside: float32 [4, 20, 65536], P(None, None, ('cols', 'rep')), may hold values from 0.001 to 1
- children: int32 [31, 2], replicated, may hold values from 0 to 61, as said below
- branch: float32 [62], replicated, may hold values from 0.02 to 0.08
- root_length: float32 [1], replicated, may hold values from 0.02 to 0.08
- cat_rates: float32 [4], replicated, may hold values from 0.1 to 2.5
- exchange_rates: float32 [20, 20], replicated, may hold values from 0.1 to 1.5
- frequencies: float32 [20], replicated, may hold values from 0.02 to 0.1
- rivals: float32 [99, 65536], P(None, ('cols', 'rep')), may hold values from -120 to -20
- pattern_idx: int32 [131072], P(('cols', 'rep')), may hold values from 0 to 127
- weights: int32 [2048, 131072], P(None, ('cols', 'rep')), may hold values from 0 to 2
Outputs:
- rell_scores: float32 [100, 2048], P(None, ('cols', 'rep'))
- pattern_loglik: float32 [65536], P(('cols', 'rep'))
- root_final: float32 [1], replicated
Inputs may be any that keep to these rules, and one draw needn't show every extreme that they name: Row r holds the children of node 32 + r; ids below 32 are taxa; every node but the root, node 62, is a child exactly once, and every child id is below its parent's. `pattern_idx`: local index of the pattern a column shows among the 128 patterns of the column's block of 256 columns.
All inputs are finite; a program needn't handle non-finite values.
Results may differ from a plain program's by a relative error of at most 0.0003.
Values sent between devices are 32-bit elements; how exact they have to be, the bound alone decides.
A program may use at most 64 MiB of HBM per device.

v0:
```python
import jax
import jax.numpy as jnp
from jax import lax
from jax.sharding import PartitionSpec as P

STATES = 20
CATS = 4
TERMS = 40
LEAVES = 32
INNER = 31
NODES = 63
NEWTON = 3


MU_RATE = 4.0
LENGTH_CAP = 2.0
highest = lax.Precision.HIGHEST


def rate_powers(exchange_rates, frequencies):
    states = exchange_rates.shape[0]
    identity = jnp.eye(states, dtype=jnp.float32)
    symmetric = 0.5 * (exchange_rates + exchange_rates.T)
    offdiag = symmetric * frequencies[None, :] * (1.0 - identity)
    generator = offdiag - jnp.diag(jnp.sum(offdiag, axis=1))
    stepping = identity + generator / MU_RATE

    def advance(current, unused):
        following = jnp.dot(current, stepping, precision=highest)
        return (following, current)

    unused_last, powers = lax.scan(advance, identity, None, length=TERMS)
    return powers


def term_weights(scaled):
    orders = jnp.arange(TERMS).astype(jnp.float32)
    logged = -scaled[..., None] + orders * jnp.log(scaled)[..., None] - lax.lgamma(orders + 1.0)
    return jnp.exp(logged)


def edge_transitions(branch, cat_rates, powers):
    mixing = term_weights(MU_RATE * branch[:, None] * cat_rates[None, :])
    return jnp.einsum("eck,kij->ecij", mixing, powers, precision=highest)


def prune_block(taxa_block, outside_block, children, transitions, powers, frequencies):
    pattern_count = taxa_block.shape[1]
    onehot = (taxa_block[:, None, :] == jnp.arange(STATES)[None, :, None]).astype(jnp.float32)
    partials = jnp.zeros((NODES, CATS, STATES, pattern_count), jnp.float32)
    partials = partials.at[:LEAVES].set(
        jnp.broadcast_to(onehot[:, None], (LEAVES, CATS, STATES, pattern_count))
    )
    log_scales = jnp.zeros((NODES, pattern_count), jnp.float32)

    def merge_step(step_index, carry):
        partials, log_scales = carry
        first_child = children[step_index, 0]
        second_child = children[step_index, 1]
        left_msg = jnp.einsum(
            "cij,cjs->cis", transitions[first_child], partials[first_child], precision=highest
        )
        right_msg = jnp.einsum(
            "cij,cjs->cis", transitions[second_child], partials[second_child], precision=highest
        )
        product = left_msg * right_msg
        largest = jnp.max(product, axis=(0, 1))
        node_id = LEAVES + step_index
        partials = partials.at[node_id].set(product / largest)
        log_scales = log_scales.at[node_id].set(
            log_scales[first_child] + log_scales[second_child] + jnp.log(largest)
        )
        return (partials, log_scales)

    partials, log_scales = lax.fori_loop(0, INNER, merge_step, (partials, log_scales))
    root_partial = partials[NODES - 1]
    weighted_outside = frequencies[None, :, None] * outside_block
    lifted = jnp.einsum("kij,cjs->ckis", powers, root_partial, precision=highest)
    moment_basis = jnp.einsum("cis,ckis->cks", weighted_outside, lifted, precision=highest)
    return (moment_basis, log_scales[NODES - 1])


def derivatives(moment_basis, length, cat_rates):
    speeds = MU_RATE * cat_rates
    mixing = term_weights(speeds * length)
    zeros_one = jnp.zeros((CATS, 1), mixing.dtype)
    shifted_once = jnp.concatenate([zeros_one, mixing[:, :-1]], axis=1)
    shifted_twice = jnp.concatenate([zeros_one, shifted_once[:, :-1]], axis=1)
    slope_terms = speeds[:, None] * (shifted_once - mixing)
    bend_terms = (speeds * speeds)[:, None] * (shifted_twice - 2.0 * shifted_once + mixing)
    stacked = jnp.stack([mixing, slope_terms, bend_terms])
    return 0.25 * jnp.einsum("nck,cks->ns", stacked, moment_basis, precision=highest)


def local_sums(values, counts):
    ratio_terms = values[1] / values[0]
    first_sum = jnp.sum(counts * ratio_terms)
    second_sum = jnp.sum(counts * (values[2] / values[0] - ratio_terms * ratio_terms))
    return (first_sum, second_sum)


def newton_update(length, first_sum, second_sum):
    proposal = length - first_sum / jnp.minimum(second_sum, -1.0)
    return jnp.clip(proposal, 0.25 * length, LENGTH_CAP)


def score_rows(scored_rows, tallies):
    return lax.dot_general(scored_rows, tallies, (((1,), (1,)), ((), ())), precision=highest)


def on_device(
    taxa_states,
    outside,
    children,
    branch,
    root_length,
    cat_rates,
    exchange_rates,
    frequencies,
    rivals,
    pattern_idx,
    weights,
):
    powers = rate_powers(exchange_rates, frequencies)
    transitions = edge_transitions(branch, cat_rates, powers)
    moment_basis, root_scale = prune_block(
        taxa_states, outside, children, transitions, powers, frequencies
    )
    pattern_count = taxa_states.shape[1]
    onehot = (pattern_idx[:, None] == jnp.arange(pattern_count)[None, :]).astype(jnp.bfloat16)
    counts = jnp.sum(onehot, axis=0, dtype=jnp.float32)
    length = root_length[0]
    for newton_step in range(NEWTON):
        values = derivatives(moment_basis, length, cat_rates)
        first_local, second_local = local_sums(values, counts)
        first_sum, second_sum = lax.psum((first_local, second_local), ("cols", "rep"))
        length = newton_update(length, first_sum, second_sum)
    final_values = derivatives(moment_basis, length, cat_rates)
    pattern_loglik = jnp.log(final_values[0]) + root_scale
    tallies = jnp.dot(weights.astype(jnp.bfloat16), onehot, preferred_element_type=jnp.float32)
    scored = jnp.concatenate([pattern_loglik[None, :], rivals], axis=0)
    partial_scores = score_rows(scored, tallies)
    column_total = weights.shape[1] * lax.axis_size("cols") * lax.axis_size("rep")
    owned = lax.psum_scatter(partial_scores, ("cols", "rep"), scatter_dimension=1, tiled=True)
    return (owned / column_total, pattern_loglik, length[None])


def solution(mesh):
    placed = (
        P(None, ("cols", "rep")),
        P(None, None, ("cols", "rep")),
        P(),
        P(),
        P(),
        P(),
        P(),
        P(),
        P(None, ("cols", "rep")),
        P(("cols", "rep")),
        P(None, ("cols", "rep")),
    )
    return jax.shard_map(
        on_device,
        mesh=mesh,
        in_specs=placed,
        out_specs=(P(None, ("cols", "rep")), P(("cols", "rep")), P()),
        check_vma=False,
    )
```

profile of v0, /device:TPU:1, one launch (start us, length us, event | category | flops | bytes accessed | tf_op | source)
XLA Modules:
  0.0 1169.9 jit_solution(10186981232040259108)
XLA Ops:
  11.9 6.6 while.32
  21.1 2.7 copy.34
  24.5 350.3 %while.33 = (s32[]{:T(128)}, f32[63,4,20,128]{3,2,1,0:T(8,128)S(1)}, f32[63,128]{1,0:T(8,128)S(1)}, s32[31,2]{0,1:T(2,128)S(1)}, f32[62,4,20,20]{3,2,1,0:T(8,128...) while((s32[]{:T(128)}, ...), condition=%wide.region_8.9_spmd, body=%wide.region_4.8_spmd.sunk | while | flops 4956468 | bytes 480141 | solution.py:75
  32.2 1.0 fusion.93
  43.5 1.0 fusion.93
  50.5 1.0 fusion.92
  54.8 1.0 fusion.93
  61.8 1.0 fusion.92
  66.1 1.0 fusion.93
  73.1 1.0 fusion.92
  77.4 1.0 fusion.93
  84.4 1.0 fusion.92
  88.7 1.0 fusion.93
  95.7 1.0 fusion.92
  100.0 1.0 fusion.93
  107.0 1.0 fusion.92
  111.3 1.0 fusion.93
  122.6 1.0 fusion.93
  133.9 1.0 fusion.93
  145.2 1.0 fusion.93
  156.5 1.0 fusion.93
  167.8 1.0 fusion.93
  179.1 1.0 fusion.93
  190.4 1.0 fusion.93
  201.7 1.0 fusion.93
  213.0 1.0 fusion.93
  224.3 1.0 fusion.93
  235.6 1.0 fusion.93
  246.9 1.0 fusion.93
  258.2 1.0 fusion.93
  269.5 1.0 fusion.93
  280.8 1.0 fusion.93
  292.1 1.0 fusion.93
  303.4 1.0 fusion.93
  314.7 1.0 fusion.93
  326.0 1.0 fusion.93
  337.3 1.0 fusion.93
  348.6 1.0 fusion.93
  359.9 1.0 fusion.93
  371.2 1.0 fusion.93
  375.9 1.5 fusion.14
  378.4 111.1 %all-reduce.12 = (f32[]{:T(128)}, f32[]{:T(128)}) all-reduce(f32[]{:T(128)} %get-tuple-element.237, f32[]{:T(128)} %get-tuple-element.236), channel_id=1, replica_groups=mesh['cols'=128,'rep'=4] {'cols','rep'}, use_global_device_ids=true, to_apply=%region_10.11 | all-reduce | flops 2 | bytes 16 | tf_op jit(solution)/shard_map/psum | solution.py:136
  492.0 98.6 %all-reduce.11 = (f32[]{:T(128)}, f32[]{:T(128)}) all-reduce(f32[]{:T(128)} %get-tuple-element.235, f32[]{:T(128)} %get-tuple-element.234), channel_id=1, replica_groups=mesh['cols'=128,'rep'=4] {'cols','rep'}, use_global_device_ids=true, to_apply=%region_14.15 | all-reduce | flops 2 | bytes 16 | tf_op jit(solution)/shard_map/psum | solution.py:136
  593.2 99.6 %all-reduce.10 = (f32[]{:T(128)}, f32[]{:T(128)}) all-reduce(f32[]{:T(128)} %get-tuple-element.233, f32[]{:T(128)} %get-tuple-element.232), channel_id=1, replica_groups=mesh['cols'=128,'rep'=4] {'cols','rep'}, use_global_device_ids=true, to_apply=%region_18.19 | all-reduce | flops 2 | bytes 16 | tf_op jit(solution)/shard_map/psum | solution.py:136
  694.7 2.2 fusion.19
  696.9 2.9 fusion.37
  699.8 460.9 %all-reduce.15.cloned.1.call-done = f32[100,2048]{0,1:T(8,128)} async-done(((f32[100,2048]{0,1:T(8,128)}), f32[100,2048]{0,1:T(8,128)}) %all-reduce.15.cloned.1.call-update) | async-done | bytes 819216
  1160.6 1.3 dynamic-slice_multiply_fusion
  (401 shorter events, 142.0 us)
Async XLA Ops:
  7.2 1153.5 %all-reduce.15.cloned.1.call-start = ((), (), s32[]{:S(2)}) async-start(), calls=%async_computation | async-start | bytes 2097152
  18.5 5.3 copy-start.2
  23.9 0.7 copy-start.1
  23.9 0.7 copy-start.4
  23.9 0.7 copy-start.5
  24.0 350.9 %copy-start.7 = (f32[20]{0:T(128)S(1)}, f32[20]{0:T(128)}, u32[]{:S(2)}) copy-start(f32[20]{0:T(128)} %param.28) | copy-start | bytes 244
  24.0 351.8 %copy-start.6 = (s32[256]{0:T(256)S(1)}, s32[256]{0:T(256)}, u32[]{:S(2)}) copy-start(s32[256]{0:T(256)} %param.30) | copy-start | bytes 3076
  24.4 466.4 %copy-start.3 = (f32[4]{0:T(128)S(1)}, f32[4]{0:T(128)}, u32[]{:S(2)}) copy-start(f32[4]{0:T(128)} %param.26) | copy-start | bytes 52
  374.9 322.0 %copy-start = (f32[99,128]{1,0:T(8,128)S(1)}, f32[99,128]{1,0:T(8,128)}, u32[]{:S(2)}) copy-start(f32[99,128]{1,0:T(8,128)} %param.29) | copy-start | bytes 152068
  696.9 465.0 %copy-start.8 = (f32[1,128]{1,0:T(1,128)}, f32[1,128]{1,0:T(1,128)S(1)}, u32[]{:S(2)}) copy-start(f32[1,128]{1,0:T(1,128)S(1)} %slice_add_fusion) | copy-start | bytes 1540
Sparse Core Ops, SparseCore 0:
  699.9 460.7 all-reduce.14
where the time goes:
time: 1180 us; the launch traced here: 1170 us
  waiting for transfers between devices  461 us (39%)
  blocking collectives  309 us (26%)
  loops' own time  189 us (16%)
  other arithmetic  88.5 us (8%)
  matrix products  77.4 us (7%)
  local copies, waits for them, and re-layouts  24.9 us (2%)
  between operations  20 us (2%)
    unnamed x2, waiting for transfers between devices  461 us
    psum x3, blocking collectives, on_device(): lax.psum((first_local, second_local), ('cols', 'rep'))  309 us
    another operation x1, loops' own time, prune_block(): lax.fori_loop(0, INNER, merge_step, (partials, log_scales))  188 us
    another operation x93, other arithmetic  61.3 us
    dot_general x31, matrix products, merge_step(): jnp.einsum('cij,cjs->cis', transitions[second_child], partials[second_chi...  32.2 us
    dot_general x31, matrix products, merge_step(): jnp.einsum('cij,cjs->cis', transitions[first_child], partials[first_child...  31.6 us
  transfers between devices with their start and end apart: 1, of which 1 were waited for; matrix products, arithmetic and copies ran while one was open for 0% of the time, Pallas kernels for 0%

commit v1 on v0

v1 whole, which is shorter than its diff:
```python
import functools
import math

import jax
import jax.numpy as jnp
import numpy as np
from jax import lax
from jax.experimental import pallas as pl
from jax.experimental.pallas import tpu as pltpu
from jax.sharding import PartitionSpec as P

STATES = 20
CATS = 4
TERMS = 40
LEAVES = 32
INNER = 31
EDGES = 62
NEWTON = 3
RIVALS = 99
CAND = 100
MU_RATE = 4.0
LENGTH_CAP = 2.0
CORES = 2
BLOCK = CATS * STATES
PAD = 24
f32 = jnp.float32
bf16 = jnp.bfloat16
MESH = pl.DeviceIdType.MESH
highest = lax.Precision.HIGHEST


def layout_of(mesh):
    cols, chips_x = mesh.shape["cols"], mesh.shape["rep"]
    chips_y = 4 if cols >= 128 else 2
    return dict(z=cols // (CORES * chips_y), y=chips_y, c=CORES, x=chips_x)


def position(dims):
    cols = lax.axis_index("cols")
    return dict(
        z=cols // (dims["y"] * dims["c"]),
        y=(cols // dims["c"]) % dims["y"],
        c=cols % dims["c"],
        x=lax.axis_index("rep"),
    )


def device_of(dims, at):
    return ((at["z"] * dims["y"] + at["y"]) * dims["c"] + at["c"], at["x"])


def group_size(dims, axes):
    return math.prod(dims[a] for a in axes)


def group_index(dims, axes, at):
    index = 0
    for a in axes:
        index = index * dims[a] + at[a]
    return index


def group_member(dims, axes, at, index):
    member = dict(at)
    for a in reversed(axes):
        member[a] = index % dims[a]
        index = index // dims[a]
    return member


def tree_sum(values):
    while len(values) > 1:
        paired = [values[i] + values[i + 1] for i in range(0, len(values) - 1, 2)]
        if len(values) % 2:
            paired.append(values[-1])
        values = paired
    return values[0]


def split_high(value):
    return value.astype(bf16).astype(f32)


def iota(shape, axis):
    return lax.broadcasted_iota(jnp.int32, shape, axis)


def pick(index, entries, base):
    chosen = base
    for number, entry in enumerate(entries):
        chosen = jnp.where(index == number, entry, chosen)
    return chosen


PLANE = ("y", "x")
COLUMN = ("z", "c")
LINE = ("z",)


def kernel(
    dims,
    lg_lane,
    lg_row,
    taxa,
    outside,
    children,
    branch,
    root_length,
    rates,
    exchange,
    freqs,
    pattern,
    rivals_hbm,
    weights_hbm,
    out_scores,
    out_loglik,
    out_root,
    w_int,
    riv,
    w_b,
    onehot_b,
    square,
    pow_a,
    pow_b,
    x_col,
    t_a,
    t_b,
    msg,
    largest_rows,
    prod_s,
    root_s,
    lhs_s,
    wo_s,
    m_s,
    score_s,
    pair_r,
    rs_a,
    rs_r1,
    rs_b,
    rs_r2,
    val_a,
    val_b,
    ar_a,
    ar_b,
    row_v,
    row_r1,
    row_u,
    row_r2,
    load_sem,
    ar_send,
    ar_recv,
    rs_send,
    rs_recv,
    row_send,
    row_recv,
):
    at = position(dims)
    reps = score_s.shape[0] * CORES * score_s.shape[2] * 8
    lanes_z = reps // dims["z"]

    barrier = pltpu.get_barrier_semaphore()
    greeted = 0
    for axes in (PLANE, COLUMN):
        size, mine = group_size(dims, axes), group_index(dims, axes, at)
        for step in range(1, size):
            peer = group_member(dims, axes, at, (mine + step) % size)
            pl.semaphore_signal(barrier, inc=1, device_id=device_of(dims, peer), device_id_type=MESH)
            greeted += 1

    weights_copy = pltpu.make_async_copy(weights_hbm, w_int, load_sem.at[0])
    rivals_copy = pltpu.make_async_copy(rivals_hbm, riv, load_sem.at[1])
    weights_copy.start()
    rivals_copy.start()

    square[...] = jnp.zeros_like(square)
    square[0:STATES, 0:STATES] = exchange[...]
    full = square[...]
    symmetric = (0.5 * (full + full.T))[0:PAD]
    row24, lane24 = iota((PAD, 128), 0), iota((PAD, 128), 1)
    freq_row = pick(iota((1, 128), 1), [freqs[j] for j in range(STATES)], jnp.zeros((1, 128), f32))
    off = jnp.where(row24 == lane24, 0.0, symmetric * freq_row)
    away = jnp.sum(off, axis=1, keepdims=True)
    inside = (row24 == lane24) & (row24 < STATES)
    eye = jnp.where(inside, 1.0, jnp.zeros((PAD, 128), f32))
    stepping = eye + (off - jnp.where(inside, away, 0.0)) / MU_RATE

    def spread(block):
        twice = block + pltpu.roll(block, 20, 1)
        four = twice + pltpu.roll(twice, 40, 1)
        low = jnp.where(lane24 < 80, four, pltpu.roll(four, 80, 1))
        return low, pltpu.roll(low, 120, 1)

    for k, block in enumerate((eye, stepping)):
        low, high = spread(block)
        pow_a[k * PAD : (k + 1) * PAD, :] = low
        pow_b[k * PAD : (k + 1) * PAD, :] = high
    reach = 1
    while reach < TERMS:
        count = min(reach + 1, TERMS - reach)
        right = jnp.concatenate(
            [pow_a[reach * PAD : (reach + 1) * PAD, :], pow_b[reach * PAD : (reach + 1) * PAD, :]], axis=1
        )
        right = jnp.concatenate([right, jnp.zeros((128 - PAD, 256), f32)], axis=0)
        product = jnp.dot(pow_a[0 : count * PAD, :], right, precision=highest, preferred_element_type=f32)
        pow_a[reach * PAD : (reach + count) * PAD, :] = product[:, 0:128]
        pow_b[reach * PAD : (reach + count) * PAD, :] = product[:, 128:256]
        reach *= 2

    row8 = iota((8, 128), 0)
    speed = [MU_RATE * rates[c] for c in range(CATS)]
    speed8 = pick(row8 % CATS, speed, jnp.zeros((8, 128), f32))
    for pair in range(EDGES // 2):
        x_col[pair * 8 : pair * 8 + 8, :] = speed8 * jnp.where(row8 < CATS, branch[2 * pair], branch[2 * pair + 1])
    x_col[EDGES * CATS :, :] = jnp.ones((8, 128), f32)
    scaled = x_col[...]
    lane1 = iota((1, 128), 1)
    part = (lane1 >= 40).astype(jnp.int32) + (lane1 >= 80).astype(jnp.int32) + (lane1 >= 120).astype(jnp.int32)
    order = (lane1 - 40 * part).astype(f32)
    mixing = jnp.exp(-scaled + order * jnp.log(scaled) - lg_lane[...])
    mixing_high = split_high(mixing)
    mixing = jnp.where(part == 2, mixing - mixing_high, jnp.where(part == 3, 0.0, mixing_high))
    mixing = mixing.astype(bf16)

    lane256 = iota((1, 256), 1)
    copy256 = (lane256 >= 80).astype(jnp.int32) + (lane256 >= 160).astype(jnp.int32) + (lane256 >= 240).astype(jnp.int32)
    within = lane256 - 80 * copy256
    cat256 = (within >= 20).astype(jnp.int32) + (within >= 40).astype(jnp.int32) + (within >= 60).astype(jnp.int32)
    cat256 = jnp.where(copy256 == 3, -1, cat256)
    keep = (iota((256, 1), 0) % CATS) == cat256
    lane128 = iota((1, 128), 1)
    lhs_part = (lane128 >= 40).astype(jnp.int32) + (lane128 >= 80).astype(jnp.int32) + (lane128 >= 100).astype(jnp.int32)
    lhs_used = (lane128 < 20) | ((lane128 >= 40) & (lane128 < 60)) | ((lane128 >= 80) & (lane128 < 100))
    for i in range(STATES):
        base_a = pow_a[pl.ds(i, TERMS, stride=PAD), :]
        base_b = pow_b[pl.ds(i, TERMS, stride=PAD), :]
        base = jnp.concatenate([base_a, base_b], axis=1)
        base_high = split_high(base)
        right = jnp.concatenate([base_high, base - base_high, base_high, jnp.zeros((8, 256), f32)], axis=0)
        made = jnp.dot(mixing, right.astype(bf16), preferred_element_type=f32)
        made_high = split_high(made)
        made = jnp.where(keep, jnp.where(copy256 == 1, made - made_high, made_high), 0.0)
        t_a[pl.ds(i, 256, stride=STATES), :] = made[:, 0:128]
        t_b[pl.ds(i, 256, stride=STATES), :] = made[:, 128:256]
        a_high = base_high[:, 0:128]
        lhs_s[i * TERMS : (i + 1) * TERMS, :] = jnp.where(
            lhs_used, jnp.where(lhs_part == 1, base_a - a_high, a_high), 0.0
        )

    state80 = iota((BLOCK, 128), 0)
    state80 = state80 - 20 * (
        (state80 >= 20).astype(jnp.int32) + (state80 >= 40).astype(jnp.int32) + (state80 >= 60).astype(jnp.int32)
    )

    def leaf_step(n, carry):
        hot = jnp.where(state80 == taxa[pl.ds(n, 1), :], 1.0, jnp.zeros((BLOCK, 128), f32)).astype(bf16)
        start = pl.multiple_of(n * BLOCK, 16)
        left = jnp.concatenate([t_a[pl.ds(start, BLOCK), :], t_b[pl.ds(start, BLOCK), 0:32]], axis=1)
        right = jnp.concatenate([hot, hot], axis=0)
        msg[n] = jnp.dot(left.astype(bf16), right, preferred_element_type=f32)
        return carry

    lax.fori_loop(0, LEAVES, leaf_step, 0, unroll=4)

    largest_rows[...] = jnp.ones_like(largest_rows)

    def merged(r):
        return msg[children[r, 0]] * msg[children[r, 1]]

    def inner_step(r, carry):
        product = merged(r)
        largest = jnp.max(product, axis=0, keepdims=True)
        largest_rows[pl.ds(r, 1), :] = largest
        high = product.astype(bf16)
        low = (product - high.astype(f32)).astype(bf16)
        right = jnp.concatenate([high, high, low, jnp.zeros((16, 128), bf16)], axis=0)
        start = pl.multiple_of((LEAVES + r) * BLOCK, 16)
        left = jnp.concatenate([t_a[pl.ds(start, BLOCK), :], t_b[pl.ds(start, BLOCK), :]], axis=1)
        moved = jnp.dot(left.astype(bf16), right, preferred_element_type=f32)
        msg[LEAVES + r] = moved * (1.0 / largest)
        return carry

    lax.fori_loop(0, INNER - 1, inner_step, 0)
    product = merged(INNER - 1)
    largest = jnp.max(product, axis=0, keepdims=True)
    largest_rows[INNER - 1 : INNER, :] = largest
    prod_s[...] = product * (1.0 / largest)
    root_scale = jnp.sum(jnp.log(largest_rows[...]), axis=0, keepdims=True)

    root_s[...] = jnp.zeros_like(root_s)
    for c in range(CATS):
        piece = prod_s[c * STATES : (c + 1) * STATES, :]
        piece_high = split_high(piece)
        root_s[0:STATES, c * 128 : (c + 1) * 128] = piece_high
        root_s[40 : 40 + STATES, c * 128 : (c + 1) * 128] = piece_high
        root_s[80 : 80 + STATES, c * 128 : (c + 1) * 128] = piece - piece_high
    freq_col = pick(iota((STATES, 128), 0), [freqs[j] for j in range(STATES)], jnp.zeros((STATES, 128), f32))
    for c in range(CATS):
        wo_s[c] = freq_col * outside[c]
    root_b = root_s[...].astype(bf16)
    lhs_b = lhs_s[...].astype(bf16)
    lifted = jnp.dot(lhs_b, root_b, preferred_element_type=f32)
    m_s[...] = jnp.zeros_like(m_s)
    for c in range(CATS):
        basis = jnp.zeros((TERMS, 128), f32)
        for i in range(STATES):
            basis = basis + lifted[i * TERMS : (i + 1) * TERMS, c * 128 : (c + 1) * 128] * wo_s[c, i : i + 1, :]
        m_s[c, 0:TERMS, :] = basis
    order_row = iota((TERMS, 128), 0).astype(f32)
    lg_rows = lg_row[...]
    basis0, basis1, basis2 = [], [], []
    for c in range(CATS):
        here, next1, next2 = m_s[c, 0:TERMS, :], m_s[c, 1 : TERMS + 1, :], m_s[c, 2 : TERMS + 2, :]
        basis0.append(here)
        basis1.append(speed[c] * (next1 - here))
        basis2.append((speed[c] * speed[c]) * (next2 - 2.0 * next1 + here))

    hot = jnp.where(iota((128, 256), 0) == pattern[...], 1.0, jnp.zeros((128, 256), f32)).astype(bf16)
    onehot_b[...] = hot
    counts = lax.dot_general(
        jnp.ones((16, 256), bf16), hot, (((1,), (1,)), ((), ())), preferred_element_type=f32
    )[0:1]

    def series(length, bases):
        totals = [jnp.zeros((TERMS, 128), f32) for _ in bases]
        for c in range(CATS):
            x = speed[c] * length
            w = jnp.exp(-x + order_row * jnp.log(x) - lg_rows)
            totals = [total + w * basis[c] for total, basis in zip(totals, bases)]
        return [0.25 * jnp.sum(total, axis=0, keepdims=True) for total in totals]

    def local_sums(length):
        value, slope, bend = series(length, (basis0, basis1, basis2))
        ratio = slope / value
        return counts * ratio, counts * (bend / value - ratio * ratio)

    def send_group(axes, source, target, send, recv):
        size, mine = group_size(dims, axes), group_index(dims, axes, at)
        for step in range(1, size):
            slot = (mine + step) % size
            peer = group_member(dims, axes, at, slot)
            pltpu.make_async_remote_copy(
                src_ref=source(slot),
                dst_ref=target.at[mine],
                send_sem=send,
                recv_sem=recv,
                device_id=device_of(dims, peer),
                device_id_type=MESH,
            ).start()

    def wait_group(target, sem):
        several = target.at[pl.ds(0, target.shape[0] - 1)]
        pltpu.make_async_copy(several, several, sem).wait()

    plane_mine, column_mine = group_index(dims, PLANE, at), group_index(dims, COLUMN, at)
    line_mine = at["z"]

    def rivals_scores():
        weights_copy.wait()
        rivals_copy.wait()
        w_b[...] = w_int[...].astype(f32).astype(bf16)
        rows = jnp.concatenate([riv[...], jnp.zeros((128 - RIVALS, 128), f32)], axis=0)
        high = rows.astype(bf16)
        low = (rows - high.astype(f32)).astype(bf16)
        both = jnp.concatenate([high, low], axis=0)
        gathered = jnp.dot(both, onehot_b[...], preferred_element_type=f32).astype(bf16)
        chunk = min(256, reps)
        for begin in range(0, reps, chunk):
            scores = lax.dot_general(
                w_b[begin : begin + chunk, :], gathered, (((1,), (1,)), ((), ())), preferred_element_type=f32
            )
            scores = scores[:, 0:128] + scores[:, 128:256]
            per = CORES * score_s.shape[2] * 8
            score_s[begin // per : (begin + chunk) // per] = scores.reshape(
                (chunk // per,) + score_s.shape[1:]
            )
        pltpu.make_async_remote_copy(
            src_ref=score_s.at[:, 1 - at["c"]],
            dst_ref=pair_r,
            send_sem=rs_send.at[0],
            recv_sem=rs_recv.at[0],
            device_id=device_of(dims, dict(at, c=1 - at["c"])),
            device_id_type=MESH,
        ).start()

    def rivals_plane():
        pltpu.make_async_copy(pair_r, pair_r, rs_recv.at[0]).wait()
        first_half = iota((1, 1, 8, 128), 2) < 4
        tiles = score_s.shape[2]
        chips_y = dims["y"]

        def pair_step(zp, carry):
            even_at = pl.ds(2 * zp * chips_y, chips_y)
            odd_at = pl.ds((2 * zp + 1) * chips_y, chips_y)
            even = score_s[even_at, at["c"]] + pair_r[even_at]
            odd = score_s[odd_at, at["c"]] + pair_r[odd_at]
            even_turned, odd_turned = pltpu.roll(even, 4, 2), pltpu.roll(odd, 4, 2)
            lower = jnp.where(first_half, even, odd_turned)
            upper = jnp.where(first_half, even_turned, odd)
            for t in range(tiles):
                rs_a[:, 2 * t, zp] = lower[:, t]
                rs_a[:, 2 * t + 1, zp] = upper[:, t]
            return carry

        lax.fori_loop(0, dims["z"] // 2, pair_step, 0)
        rs_r1[plane_mine] = rs_a[at["y"], at["x"]]
        send_group(
            PLANE,
            lambda slot: rs_a.at[slot // dims["x"], slot % dims["x"]],
            rs_r1,
            rs_send.at[1],
            rs_recv.at[1],
        )

    def rivals_line():
        wait_group(rs_r1, rs_recv.at[1])
        rs_b[...] = tree_sum([rs_r1[k] for k in range(rs_r1.shape[0])])
        rs_r2[line_mine] = rs_b[at["z"] // 2]
        send_group(LINE, lambda slot: rs_b.at[slot // 2], rs_r2, rs_send.at[2], rs_recv.at[2])

    columns_total = float(pattern.shape[1] * dims["z"] * dims["y"] * dims["c"] * dims["x"])

    def rivals_finish():
        wait_group(rs_r2, rs_recv.at[2])
        total = tree_sum([rs_r2[k] for k in range(rs_r2.shape[0])]) / columns_total
        square[...] = jnp.zeros_like(square)
        square[0:8, :] = total
        turned = square[...].T
        turned = jnp.where(at["z"] % 2 == 0, turned, pltpu.roll(turned, 124, 1))
        out_scores[1:CAND, :] = turned[0:RIVALS, 0:4]

    pl.semaphore_wait(barrier, greeted)
    length = jnp.full((1, 128), root_length[0], f32)
    hidden = [(rivals_scores, rivals_plane), (rivals_line, rivals_finish), (None, None)]
    for step in range(NEWTON):
        first, second = local_sums(length)
        val_a[step, 0:1, :] = first
        val_a[step, 1:2, :] = second
        ar_a[step, plane_mine] = val_a[step]
        send_group(PLANE, lambda slot: val_a.at[step], ar_a.at[step], ar_send.at[step, 0], ar_recv.at[step, 0])
        if hidden[step][0] is not None:
            hidden[step][0]()
        wait_group(ar_a.at[step], ar_recv.at[step, 0])
        val_b[step] = tree_sum([ar_a[step, k] for k in range(ar_a.shape[1])])
        ar_b[step, column_mine] = val_b[step]
        send_group(COLUMN, lambda slot: val_b.at[step], ar_b.at[step], ar_send.at[step, 1], ar_recv.at[step, 1])
        if hidden[step][1] is not None:
            hidden[step][1]()
        wait_group(ar_b.at[step], ar_recv.at[step, 1])
        sums = tree_sum([ar_b[step, k] for k in range(ar_b.shape[1])])
        sums = jnp.sum(sums, axis=1, keepdims=True)
        proposal = length - sums[0:1] / jnp.minimum(sums[1:2], -1.0)
        length = jnp.clip(proposal, 0.25 * length, LENGTH_CAP)
    out_root[...] = length

    (value,) = series(length, (basis0,))
    loglik = jnp.log(value) + root_scale
    out_loglik[...] = loglik
    high = split_high(loglik)
    middle = split_high(loglik - high)
    low = loglik - high - middle
    row16 = iota((16, 128), 0)
    parts = pick(row16, [high, middle, low], jnp.zeros((16, 128), f32)).astype(bf16)
    gathered = jnp.dot(parts, onehot_b[...], preferred_element_type=f32).astype(bf16)
    own = lax.dot_general(gathered, w_b[...], (((1,), (1,)), ((), ())), preferred_element_type=f32)
    own = jnp.sum(own, axis=0, keepdims=True)
    if lanes_z != 128:
        row_v[...] = jnp.zeros_like(row_v)
    for z in range(dims["z"]):
        row_v[z, :, 0:lanes_z] = own[:, z * lanes_z : (z + 1) * lanes_z]
    row_r1[column_mine] = row_v[at["z"]]
    send_group(COLUMN, lambda slot: row_v.at[slot // dims["c"]], row_r1, row_send.at[0], row_recv.at[0])
    wait_group(row_r1, row_recv.at[0])
    row_u[...] = tree_sum([row_r1[k] for k in range(row_r1.shape[0])])
    row_r2[plane_mine] = row_u[...]
    send_group(PLANE, lambda slot: row_u, row_r2, row_send.at[1], row_recv.at[1])
    wait_group(row_r2, row_recv.at[1])
    total = tree_sum([row_r2[k] for k in range(row_r2.shape[0])]) / columns_total
    shift = ((at["y"] * dims["c"] + at["c"]) * dims["x"] + at["x"]) * 4
    total = pltpu.roll(jnp.broadcast_to(total, (8, 128)), 128 - shift, 1)
    out_scores[0:1, :] = total[0:1, 0:4]

    for step in range(NEWTON):
        wait_group(ar_a.at[step], ar_send.at[step, 0])
        wait_group(ar_b.at[step], ar_send.at[step, 1])
    pltpu.make_async_copy(pair_r, pair_r, rs_send.at[0]).wait()
    wait_group(rs_r1, rs_send.at[1])
    wait_group(rs_r2, rs_send.at[2])
    wait_group(row_r1, row_send.at[0])
    wait_group(row_r2, row_send.at[1])


def on_device(
    dims,
    taxa_states,
    outside,
    children,
    branch,
    root_length,
    cat_rates,
    exchange_rates,
    frequencies,
    rivals,
    pattern_idx,
    weights,
):
    reps, columns = weights.shape
    patterns = taxa_states.shape[1]
    z, y, c, x = (dims[a] for a in ("z", "y", "c", "x"))
    tiles = x // 2
    plane, column = group_size(dims, PLANE), group_size(dims, COLUMN)
    log_factorials = np.array([math.lgamma(k + 1.0) for k in range(TERMS)], np.float32)
    lg_lane = np.zeros((1, 128), np.float32)
    for part in range(3):
        lg_lane[0, part * TERMS : (part + 1) * TERMS] = log_factorials
    lg_row = np.broadcast_to(log_factorials[:, None], (TERMS, 128))
    vmem = pl.BlockSpec(memory_space=pltpu.VMEM)
    smem = pl.BlockSpec(memory_space=pltpu.SMEM)
    hbm = pl.BlockSpec(memory_space=pl.ANY)
    scores, loglik, root = pl.pallas_call(
        functools.partial(kernel, dims),
        out_shape=(
            jax.ShapeDtypeStruct((CAND, 4), f32),
            jax.ShapeDtypeStruct((1, patterns), f32),
            jax.ShapeDtypeStruct((1, 128), f32),
        ),
        in_specs=[vmem, vmem, vmem, vmem, smem, smem, smem, smem, vmem, smem, vmem, hbm, hbm],
        out_specs=(vmem, vmem, vmem),
        scratch_shapes=[
            pltpu.VMEM((reps, columns), jnp.int32),
            pltpu.VMEM((RIVALS, 128), f32),
            pltpu.VMEM((reps, columns), bf16),
            pltpu.VMEM((128, columns), bf16),
            pltpu.VMEM((128, 128), f32),
            pltpu.VMEM((TERMS * PAD, 128), f32),
            pltpu.VMEM((TERMS * PAD, 128), f32),
            pltpu.VMEM((256, 128), f32),
            pltpu.VMEM((256 * STATES, 128), f32),
            pltpu.VMEM((256 * STATES, 128), f32),
            pltpu.VMEM((EDGES, BLOCK, 128), f32),
            pltpu.VMEM((32, 128), f32),
            pltpu.VMEM((BLOCK, 128), f32),
            pltpu.VMEM((128, CATS * 128), f32),
            pltpu.VMEM((STATES * TERMS, 128), f32),
            pltpu.VMEM((CATS, STATES, 128), f32),
            pltpu.VMEM((CATS, TERMS + 8, 128), f32),
            pltpu.VMEM((z * y, c, tiles, 8, 128), f32),
            pltpu.VMEM((z * y, tiles, 8, 128), f32),
            pltpu.VMEM((y, x, z // 2, 8, 128), f32),
            pltpu.VMEM((plane, z // 2, 8, 128), f32),
            pltpu.VMEM((z // 2, 8, 128), f32),
            pltpu.VMEM((z, 8, 128), f32),
            pltpu.VMEM((NEWTON, 2, 128), f32),
            pltpu.VMEM((NEWTON, 2, 128), f32),
            pltpu.VMEM((NEWTON, plane, 2, 128), f32),
            pltpu.VMEM((NEWTON, column, 2, 128), f32),
            pltpu.VMEM((z, 1, 128), f32),
            pltpu.VMEM((column, 1, 128), f32),
            pltpu.VMEM((1, 128), f32),
            pltpu.VMEM((plane, 1, 128), f32),
            pltpu.SemaphoreType.DMA((2,)),
            pltpu.SemaphoreType.DMA((NEWTON, 2)),
            pltpu.SemaphoreType.DMA((NEWTON, 2)),
            pltpu.SemaphoreType.DMA((3,)),
            pltpu.SemaphoreType.DMA((3,)),
            pltpu.SemaphoreType.DMA((2,)),
            pltpu.SemaphoreType.DMA((2,)),
        ],
        compiler_params=pltpu.CompilerParams(
            collective_id=0, has_side_effects=True, vmem_limit_bytes=48 * 1024 * 1024
        ),
    )(
        lg_lane,
        lg_row,
        taxa_states,
        outside,
        children,
        branch,
        root_length,
        cat_rates,
        exchange_rates,
        frequencies,
        pattern_idx.reshape(1, columns),
        rivals,
        weights,
    )
    return scores, loglik.reshape(patterns), root[0, 0:1]


def solution(mesh):
    placed = (
        P(None, ("cols", "rep")),
        P(None, None, ("cols", "rep")),
        P(),
        P(),
        P(),
        P(),
        P(),
        P(),
        P(None, ("cols", "rep")),
        P(("cols", "rep")),
        P(None, ("cols", "rep")),
    )
    return jax.shard_map(
        functools.partial(on_device, layout_of(mesh)),
        mesh=mesh,
        in_specs=placed,
        out_specs=(P(None, ("cols", "rep")), P(("cols", "rep")), P()),
        check_vma=False,
    )
```

time: 1180 us -> 84.1 us (0.07)
  waiting for transfers between devices: 461 us -> 0 us
  blocking collectives: 309 us -> 0 us
  loops' own time: 189 us -> 0 us
  other arithmetic: 88.5 us -> 0 us
  matrix products: 77.4 us -> 0 us
  Pallas kernels: 0 us -> 70.6 us
  between operations: 20 us -> 2.46 us
  local copies, waits for them, and re-layouts: 24.9 us -> 10.6 us
    unnamed x2 -> x0, waiting for transfers between devices: 461 us -> none
    psum x3 -> x0, blocking collectives: 309 us -> none  [on_device(): lax.psum((first_local, second_local), ('cols', 'rep'))]
    another operation x2 -> x0, loops' own time: 189 us -> none  [the longest x1 188 us: prune_block(): lax.fori_loop(0, INNER, merge_step, (partials, log_scales))]
    dot_general x110 -> x0, matrix products: 77.4 us -> none  [the longest x31 32.2 us: merge_step(): jnp.einsum('cij,cjs->cis', transitions[second_child], partials[second_chi...]
    pallas_call x0 -> x1, Pallas kernels: none -> 70.6 us  [on_device(): pl.pallas_call(functools.partial(kernel, dims), out_shape=(jax.ShapeDtype...]
    another operation x100 -> x0, other arithmetic: 61.6 us -> none
    dynamic_slice x31 -> x0, local copies, waits for them, and re-layouts: 18.2 us -> none  [merge_step(): second_child = children[step_index, 1]]
    scatter x31 -> x0, other arithmetic: 17.6 us -> none  [merge_step(): partials = partials.at[node_id].set(product / largest)]
  transfers between devices with their start and end apart: 1 -> 0, of which waited for: 1 -> 0; matrix products, arithmetic and copies ran while one was open for 0% -> 0% of each run, Pallas kernels for 0% -> 0%
where the time goes in v1:
time: 84.1 us; the launch traced here: 83.7 us
  Pallas kernels  70.6 us (84%)
  local copies, waits for them, and re-layouts  10.6 us (13%)
  between operations  2.46 us (3%)
    pallas_call x1, Pallas kernels, on_device(): pl.pallas_call(functools.partial(kernel, dims), out_shape=(jax.ShapeDtype...  70.6 us
    unnamed x22, local copies, waits for them, and re-layouts  9.84 us

profile of v1, /device:TPU:1, one launch (start us, length us, event | category | flops | bytes accessed | tf_op | source)
XLA Modules:
  0.0 83.7 jit_solution(18024012304482466791)
XLA Ops:
  1.3 0.8 copy.17.children
  2.0 0.8 copy.16.outside
  2.8 0.7 jit_solution_.3.lg_row
  3.6 0.0 copy-start
  3.6 1.6 %copy-done = s32[2048,256]{1,0:T(8,128)S(1)} copy-done((s32[2048,256]{1,0:T(8,128)S(1)}, s32[2048,256]{1,0:T(8,128)}, u32[]{:S(2)}) %copy-start) | copy-done | bytes 2097176
  5.2 0.0 copy-start.1
  5.2 0.8 copy-done.1
  6.0 0.0 copy-start.2
  6.0 0.7 copy-done.2
  6.7 0.0 copy-start.3
  6.7 0.7 copy-done.3
  7.4 0.0 copy-start.4
  7.4 0.7 copy-done.4
  8.1 0.0 copy-start.5
  8.1 0.7 copy-done.5
  8.7 0.0 copy-start.6
  8.7 0.7 copy-done.6
  9.4 0.0 copy-start.7
  9.4 0.7 copy-done.7
  10.0 0.0 copy-start.8
  10.0 0.7 copy-done.8
  10.7 70.6 %shard_map.148 = (f32[100,4]{1,0:T(8,128)S(1)}, f32[1,128]{1,0:T(1,128)S(1)}, f32[1,128]{1,0:T(1,128)S(1)}) custom-call(f32[1,128]{1,0:T(1,128)S(1)} %copy-done.8, f32[40,128]{1,0:T(8,128)S(1)} %jit_solution_.3.lg_row, s32[32,128]{1,0:T(8,128)S(1)} %copy-done.2, f32[4,20,128]{2,1,0:T(8,128)S(1)} %copy.16.outside, s32[31,2]{1,0:T(8,128)S(1)} %copy.17.children, ...), custom_call_target="tpu_custom_call" | custom-call | tf_op jit(solution)/shard_map/pallas_call | solution.py:519
  81.3 0.7 copy.18
  82.0 0.5 copy.22
Async XLA Ops:
  3.6 1.6 %copy-start = (s32[2048,256]{1,0:T(8,128)S(1)}, s32[2048,256]{1,0:T(8,128)}, u32[]{:S(2)}) copy-start(s32[2048,256]{1,0:T(8,128)} %weights_hbm.1) | copy-start | bytes 6291460
  5.2 0.8 copy-start.1
  6.0 0.7 copy-start.2
  6.7 0.7 copy-start.3
  7.4 0.7 copy-start.4
  8.1 0.7 copy-start.5
  8.7 0.7 copy-start.6
  9.4 0.7 copy-start.7
  10.0 0.7 copy-start.8

commit v2 on v1

v2 whole, which is shorter than its diff:
```python
import functools
import math

import jax
import jax.numpy as jnp
from jax import lax
from jax.experimental import pallas as pl
from jax.experimental.pallas import tpu as pltpu
from jax.sharding import PartitionSpec as P

STATES = 20
CATS = 4
TERMS = 40
LEAVES = 32
INNER = 31
EDGES = 62
NEWTON = 3
RIVALS = 99
CAND = 100
MU_RATE = 4.0
LENGTH_CAP = 2.0
CORES = 2
BLOCK = CATS * STATES
PAD = 24
f32 = jnp.float32
bf16 = jnp.bfloat16
LOG_FACTORIALS = [math.lgamma(k + 1.0) for k in range(TERMS)]
MESH = pl.DeviceIdType.MESH
LEAF_UNROLL = 32
DIRECT_SLACK = 2
LEVELS = DIRECT_SLACK + 1
INNER_UNROLL = 1


def layout_of(mesh):
    cols, chips_x = mesh.shape["cols"], mesh.shape["rep"]
    chips_y = 4 if cols >= 128 else 2
    return dict(z=cols // (CORES * chips_y), y=chips_y, c=CORES, x=chips_x)


def position(dims):
    cols = lax.axis_index("cols")
    return dict(
        z=cols // (dims["y"] * dims["c"]),
        y=(cols // dims["c"]) % dims["y"],
        c=cols % dims["c"],
        x=lax.axis_index("rep"),
    )


def device_of(dims, at):
    return ((at["z"] * dims["y"] + at["y"]) * dims["c"] + at["c"], at["x"])


def group_size(dims, axes):
    return math.prod(dims[a] for a in axes)


def group_index(dims, axes, at):
    index = 0
    for a in axes:
        index = index * dims[a] + at[a]
    return index


def group_member(dims, axes, at, index):
    member = dict(at)
    for a in reversed(axes):
        member[a] = index % dims[a]
        index = index // dims[a]
    return member


def tree_sum(values):
    while len(values) > 1:
        paired = [values[i] + values[i + 1] for i in range(0, len(values) - 1, 2)]
        if len(values) % 2:
            paired.append(values[-1])
        values = paired
    return values[0]


def split_high(value):
    return value.astype(bf16).astype(f32)


def iota(shape, axis):
    return lax.broadcasted_iota(jnp.int32, shape, axis)


def pick(index, entries, base):
    chosen = base
    for number, entry in enumerate(entries):
        chosen = jnp.where(index == number, entry, chosen)
    return chosen


def ring(step, size):
    return min(step, size - step)


def routes(dims):
    plane = sorted(
        ((ring(dy, dims["y"]) + ring(dx, dims["x"]), dy, dx) for dy in range(dims["y"]) for dx in range(dims["x"]))
    )
    column = sorted(((ring(dz, dims["z"]), dz, flip) for dz in range(dims["z"]) for flip in range(dims["c"])))
    most = plane[-1][0] + column[-1][0] - DIRECT_SLACK
    direct = [
        (dz, flip, dy, dx)
        for far, dz, flip in reversed(column)
        for wide, dy, dx in reversed(plane)
        if far > 0 and wide > 0 and far + wide > most
    ]

    def reach(here, limits):
        return max(other for other in limits if here == 0 or other == 0 or here + other <= most)

    wides, fars = sorted({p[0] for p in plane}), sorted({p[0] for p in column})
    column_needs = {far: reach(far, wides) for far in fars}
    plane_needs = {wide: reach(wide, fars) for wide in wides}
    return plane, column, direct, column_needs, plane_needs


PLANE = ("y", "x")
COLUMN = ("z", "c")
LINE = ("z",)


def kernel(
    dims,
    taxa_hbm,
    outside_hbm,
    children_hbm,
    branch_hbm,
    root_length_hbm,
    rates_hbm,
    exchange_hbm,
    freqs_hbm,
    pattern_hbm,
    rivals_hbm,
    weights_hbm,
    out_scores,
    out_loglik,
    out_root,
    taxa,
    outside,
    children,
    branch,
    root_length,
    rates,
    exchange,
    freqs,
    pattern,
    w_int,
    riv,
    w_b,
    onehot_b,
    square,
    powers,
    x_col,
    t_leaf,
    t_high,
    t_low,
    msg,
    largest_rows,
    prod_s,
    root_s,
    lhs_s,
    wo_s,
    m_s,
    score_s,
    pair_r,
    rs_a,
    rs_r1,
    rs_b,
    rs_r2,
    val_a,
    val_b,
    ar_a,
    ar_b,
    ar_d,
    row_v,
    row_r1,
    row_u,
    row_r2,
    row_d,
    root_a,
    root_b,
    root_c,
    root_m,
    load_sem,
    ar_send,
    ar_recv,
    rs_send,
    rs_recv,
    row_send,
    row_recv,
    root_send,
    root_recv,
):
    at = position(dims)
    reps = score_s.shape[0] * CORES * score_s.shape[2] * 8
    lanes_z = reps // dims["z"]

    loads = {}
    for number, (name, source, target) in enumerate(
        (
            ("exchange", exchange_hbm, exchange),
            ("freqs", freqs_hbm, freqs),
            ("rates", rates_hbm, rates),
            ("branch", branch_hbm, branch),
            ("taxa", taxa_hbm, taxa),
            ("children", children_hbm, children),
            ("root", root_length_hbm, root_length),
            ("outside", outside_hbm, outside),
            ("pattern", pattern_hbm, pattern),
            ("weights", weights_hbm, w_int),
            ("rivals", rivals_hbm, riv),
        )
    ):
        loads[name] = pltpu.make_async_copy(source, target, load_sem.at[number])
        loads[name].start()

    plane_offsets, column_offsets, direct_offsets, column_needs, plane_needs = routes(dims)

    def peer_at(dz=0, flip=0, dy=0, dx=0):
        core = at["c"] if flip == 0 else 1 - at["c"]
        there = dict(z=(at["z"] + dz) % dims["z"], c=core, y=(at["y"] + dy) % dims["y"], x=(at["x"] + dx) % dims["x"])
        return there, device_of(dims, there)

    barrier = pltpu.get_barrier_semaphore()
    greeted = [peer_at(dz, flip)[1] for _, dz, flip in column_offsets[1:]]
    greeted += [peer_at(dy=dy, dx=dx)[1] for _, dy, dx in plane_offsets[1:]]
    greeted += [peer_at(*offset)[1] for offset in direct_offsets]
    for device in greeted:
        pl.semaphore_signal(barrier, inc=1, device_id=device, device_id_type=MESH)

    square[...] = jnp.zeros_like(square)
    loads["exchange"].wait()
    loads["freqs"].wait()
    square[0:STATES, 0:STATES] = exchange[...]
    full = square[...]
    symmetric = (0.5 * (full + full.T))[0:PAD]
    row24, lane24 = iota((PAD, 128), 0), iota((PAD, 128), 1)
    freq_row = pick(iota((1, 128), 1), [freqs[j] for j in range(STATES)], jnp.zeros((1, 128), f32))
    off = jnp.where(row24 == lane24, 0.0, symmetric * freq_row)
    away = jnp.sum(off, axis=1, keepdims=True)
    inside = (row24 == lane24) & (row24 < STATES)
    eye = jnp.where(inside, 1.0, jnp.zeros((PAD, 128), f32))
    stepping = eye + (off - jnp.where(inside, away, 0.0)) / MU_RATE

    def spread(block):
        twice = block + pltpu.roll(block, 20, 1)
        four = twice + pltpu.roll(twice, 40, 1)
        return jnp.where(lane24 < 80, four, pltpu.roll(four, 80, 1))

    def three_parts(value):
        high = split_high(value)
        middle = split_high(value - high)
        return high, middle, value - high - middle

    powers[0:PAD, :] = spread(eye)
    powers[PAD : 2 * PAD, :] = spread(stepping)
    lane1 = iota((1, 128), 1)
    reach = 1
    while reach < TERMS:
        count = min(reach + 1, TERMS - reach)
        high, middle, low = three_parts(powers[reach * PAD : (reach + 1) * PAD, :])
        for slot, piece in enumerate((high, middle, low, high, middle, high)):
            square[slot * STATES : (slot + 1) * STATES, :] = piece[0:STATES]
        square[120:128, :] = jnp.zeros((8, 128), f32)
        high, middle, low = three_parts(powers[0 : count * PAD, :])
        left = jnp.where(lane1 < 60, high, jnp.where(lane1 < 100, middle, jnp.where(lane1 < 120, low, 0.0)))
        powers[reach * PAD : (reach + count) * PAD, :] = jnp.dot(
            left.astype(bf16), square[...].astype(bf16), preferred_element_type=f32
        )
        reach *= 2

    loads["rates"].wait()
    loads["branch"].wait()
    row8 = iota((8, 128), 0)
    speed = [MU_RATE * rates[c] for c in range(CATS)]
    speed8 = pick(row8 % CATS, speed, jnp.zeros((8, 128), f32))
    for pair in range(EDGES // 2):
        x_col[pair * 8 : pair * 8 + 8, :] = speed8 * jnp.where(row8 < CATS, branch[2 * pair], branch[2 * pair + 1])
    x_col[EDGES * CATS :, :] = jnp.ones((8, 128), f32)
    scaled = x_col[...]
    part = (lane1 >= 40).astype(jnp.int32) + (lane1 >= 80).astype(jnp.int32) + (lane1 >= 120).astype(jnp.int32)
    order = lane1 - 40 * part
    lg_lane = pick(order, LOG_FACTORIALS, jnp.zeros((1, 128), f32))
    order = order.astype(f32)
    mixing = jnp.exp(-scaled + order * jnp.log(scaled) - lg_lane)
    mixing_high = split_high(mixing)
    mixing = jnp.where(part == 2, mixing - mixing_high, jnp.where(part == 3, 0.0, mixing_high))
    mixing = mixing.astype(bf16)

    cat128 = (lane1 >= 20).astype(jnp.int32) + (lane1 >= 40).astype(jnp.int32) + (lane1 >= 60).astype(jnp.int32)
    cat128 = jnp.where(lane1 < BLOCK, cat128, -1)
    keep = (iota((128, 1), 0) % CATS) == cat128
    lhs_part = (lane1 >= 40).astype(jnp.int32)
    lhs_part = lhs_part + (lane1 >= 80).astype(jnp.int32)
    lhs_used = (lane1 < 20) | ((lane1 >= 40) & (lane1 < 60)) | ((lane1 >= 80) & (lane1 < 100))
    for i in range(STATES):
        base = powers[pl.ds(i, TERMS, stride=PAD), :]
        base_high = split_high(base)
        base_low = base - base_high
        right = jnp.concatenate([base_high, base_low, base_high, jnp.zeros((8, 128), f32)], axis=0)
        made = jnp.dot(mixing, right.astype(bf16), preferred_element_type=f32)
        made_high = split_high(made)
        made_low = made - made_high
        t_leaf[pl.ds(i, 128, stride=STATES), :] = jnp.where(
            lane1 < 20, made_high[0:128], jnp.where(lane1 < 40, made_low[0:128], 0.0)
        )
        t_high[pl.ds(i, 128, stride=STATES), :] = jnp.where(keep, made_high[128:256], 0.0)
        t_low[pl.ds(i, 128, stride=STATES), :] = jnp.where(keep, made_low[128:256], 0.0)
        lhs_s[i * TERMS : (i + 1) * TERMS, :] = jnp.where(
            lhs_used, jnp.where(lhs_part == 1, base_low, base_high), 0.0
        )

    state48 = iota((48, 128), 0)
    state48 = jnp.where(state48 < 20, state48, jnp.where(state48 < 40, state48 - 20, -1))
    loads["taxa"].wait()

    def leaf_step(n, carry):
        hot = jnp.where(state48 == taxa[pl.ds(n, 1), :], 1.0, jnp.zeros((48, 128), f32)).astype(bf16)
        start = pl.multiple_of(n * BLOCK, 16)
        left = t_leaf[pl.ds(start, BLOCK), 0:48]
        msg[n] = jnp.dot(left.astype(bf16), hot, preferred_element_type=f32)
        return carry

    lax.fori_loop(0, LEAVES, leaf_step, 0, unroll=LEAF_UNROLL)

    largest_rows[...] = jnp.ones_like(largest_rows)
    loads["children"].wait()

    def merged(r):
        return msg[children[0, r]] * msg[children[1, r]]

    def inner_step(r, carry):
        product = merged(r)
        largest = jnp.max(product, axis=0, keepdims=True)
        largest_rows[pl.ds(r, 1), :] = largest
        high = product.astype(bf16)
        low = (product - high.astype(f32)).astype(bf16)
        start = pl.multiple_of(r * BLOCK, 16)
        left_high = t_high[pl.ds(start, BLOCK), 0:BLOCK].astype(bf16)
        left_low = t_low[pl.ds(start, BLOCK), 0:BLOCK].astype(bf16)
        both = jnp.dot(jnp.concatenate([left_high, left_low], axis=0), high, preferred_element_type=f32)
        rest = jnp.dot(left_high, low, preferred_element_type=f32)
        moved = both[0:BLOCK] + both[BLOCK:] + rest
        msg[LEAVES + r] = moved * (1.0 / largest)
        return carry

    lax.fori_loop(0, INNER - 1, inner_step, 0, unroll=INNER_UNROLL)
    product = merged(INNER - 1)
    largest = jnp.max(product, axis=0, keepdims=True)
    largest_rows[INNER - 1 : INNER, :] = largest
    prod_s[...] = product * (1.0 / largest)
    root_scale = jnp.sum(jnp.log(largest_rows[...]), axis=0, keepdims=True)

    root_s[...] = jnp.zeros_like(root_s)
    for c in range(CATS):
        piece = prod_s[c * STATES : (c + 1) * STATES, :]
        piece_high = split_high(piece)
        root_s[0:STATES, c * 128 : (c + 1) * 128] = piece_high
        root_s[40 : 40 + STATES, c * 128 : (c + 1) * 128] = piece_high
        root_s[80 : 80 + STATES, c * 128 : (c + 1) * 128] = piece - piece_high
    loads["outside"].wait()
    for i in range(STATES):
        wo_s[i] = freqs[i] * outside[i]
    root_parts = root_s[...].astype(bf16)
    lhs_b = lhs_s[...].astype(bf16)
    lifted = jnp.dot(lhs_b, root_parts, preferred_element_type=f32)
    m_s[...] = jnp.zeros_like(m_s)
    for c in range(CATS):
        basis = jnp.zeros((TERMS, 128), f32)
        for i in range(STATES):
            basis = basis + lifted[i * TERMS : (i + 1) * TERMS, c * 128 : (c + 1) * 128] * wo_s[i, c : c + 1, :]
        m_s[c, 0:TERMS, :] = basis
    order_row = iota((TERMS, 128), 0).astype(f32)
    lg_rows = jnp.concatenate(
        [pick(row8, LOG_FACTORIALS[k : k + 8], jnp.zeros((8, 128), f32)) for k in range(0, TERMS, 8)], axis=0
    )
    basis0, basis1, basis2 = [], [], []
    for c in range(CATS):
        here, next1, next2 = m_s[c, 0:TERMS, :], m_s[c, 1 : TERMS + 1, :], m_s[c, 2 : TERMS + 2, :]
        basis0.append(here)
        basis1.append(speed[c] * (next1 - here))
        basis2.append((speed[c] * speed[c]) * (next2 - 2.0 * next1 + here))

    loads["pattern"].wait()
    loads["root"].wait()
    hot = jnp.where(iota((128, 256), 0) == pattern[...], 1.0, jnp.zeros((128, 256), f32)).astype(bf16)
    onehot_b[...] = hot
    counts = lax.dot_general(
        jnp.ones((16, 256), bf16), hot, (((1,), (1,)), ((), ())), preferred_element_type=f32
    )[0:1]

    def series(length, bases):
        totals = [jnp.zeros((TERMS, 128), f32) for _ in bases]
        for c in range(CATS):
            x = speed[c] * length
            w = jnp.exp(-x + order_row * jnp.log(x) - lg_rows)
            totals = [total + w * basis[c] for total, basis in zip(totals, bases)]
        return [0.25 * jnp.sum(total, axis=0, keepdims=True) for total in totals]

    def local_sums(length):
        value, slope, bend = series(length, (basis0, basis1, basis2))
        ratio = slope / value
        return counts * ratio, counts * (bend / value - ratio * ratio)

    def send_group(axes, source, target, send, recv):
        size, mine = group_size(dims, axes), group_index(dims, axes, at)
        for step in range(1, size):
            slot = (mine + step) % size
            peer = group_member(dims, axes, at, slot)
            pltpu.make_async_remote_copy(
                src_ref=source(slot),
                dst_ref=target.at[mine],
                send_sem=send,
                recv_sem=recv,
                device_id=device_of(dims, peer),
                device_id_type=MESH,
            ).start()

    def wait_group(target, sem):
        several = target.at[pl.ds(0, target.shape[0] - 1)]
        pltpu.make_async_copy(several, several, sem).wait()

    def send(source, target, send_sem, recv_sem, device):
        pltpu.make_async_remote_copy(
            src_ref=source,
            dst_ref=target,
            send_sem=send_sem,
            recv_sem=recv_sem,
            device_id=device,
            device_id_type=MESH,
        ).start()

    def wait_for(target, sem):
        pltpu.make_async_copy(target, target, sem).wait()

    def relay(offsets, heard, heard_sems, own, needs, forward):
        total, begin = own, 1
        for level, reach in enumerate(sorted(set(needs.values()))):
            end = sum(1 for offset in offsets if offset[0] <= reach)
            if end > begin:
                wait_for(heard.at[pl.ds(begin, end - begin)], heard_sems.at[level])
                total = total + tree_sum([heard[k] for k in range(begin, end)])
                begin = end
            forward(level, [distance for distance, needed in needs.items() if needed == reach], total)
        return total

    def level_of(distance, needs):
        return min(level for level, reach in enumerate(sorted(set(needs.values()))) if distance <= reach)

    def all_sum(step, row, meanwhile, meanwhile_later):
        sems_s, sems_r = ar_send.at[step], ar_recv.at[step]
        val_a[step] = row
        for slot, (wide, dy, dx) in reversed(list(enumerate(plane_offsets))[1:]):
            level = level_of(wide, column_needs)
            send(val_a.at[step], ar_a.at[step, slot], sems_s.at[0], sems_r.at[level], peer_at(dy=dy, dx=dx)[1])
        for slot, offset in enumerate(direct_offsets):
            send(val_a.at[step], ar_d.at[step, slot], sems_s.at[1], sems_r.at[LEVELS], peer_at(*offset)[1])
        meanwhile()

        def forward(level, distances, total):
            val_b[step, level] = total
            for slot, (far, dz, flip) in reversed(list(enumerate(column_offsets))[1:]):
                if far in distances:
                    send(
                        val_b.at[step, level],
                        ar_b.at[step, slot],
                        sems_s.at[2],
                        sems_r.at[LEVELS + 1],
                        peer_at(dz, flip)[1],
                    )

        total = relay(plane_offsets, ar_a.at[step], sems_r, row, column_needs, forward)
        meanwhile_later()
        wait_for(ar_d.at[step], sems_r.at[LEVELS])
        total = total + tree_sum([ar_d[step, k] for k in range(len(direct_offsets))])
        others = len(column_offsets) - 1
        wait_for(ar_b.at[step, pl.ds(1, others)], sems_r.at[LEVELS + 1])
        return total + tree_sum([ar_b[step, k] for k in range(1, others + 1)])

    plane_mine = group_index(dims, PLANE, at)
    line_mine = at["z"]

    def rivals_scores():
        loads["weights"].wait()
        loads["rivals"].wait()
        w_b[...] = w_int[...].astype(f32).astype(bf16)
        rows = jnp.concatenate([riv[...], jnp.zeros((128 - RIVALS, 128), f32)], axis=0)
        high = rows.astype(bf16)
        low = (rows - high.astype(f32)).astype(bf16)
        both = jnp.concatenate([high, low], axis=0)
        gathered = jnp.dot(both, onehot_b[...], preferred_element_type=f32).astype(bf16)
        chunk = min(256, reps)
        for begin in range(0, reps, chunk):
            scores = lax.dot_general(
                w_b[begin : begin + chunk, :], gathered, (((1,), (1,)), ((), ())), preferred_element_type=f32
            )
            scores = scores[:, 0:128] + scores[:, 128:256]
            per = CORES * score_s.shape[2] * 8
            score_s[begin // per : (begin + chunk) // per] = scores.reshape(
                (chunk // per,) + score_s.shape[1:]
            )
        pltpu.make_async_remote_copy(
            src_ref=score_s.at[:, 1 - at["c"]],
            dst_ref=pair_r,
            send_sem=rs_send.at[0],
            recv_sem=rs_recv.at[0],
            device_id=device_of(dims, dict(at, c=1 - at["c"])),
            device_id_type=MESH,
        ).start()

    def rivals_plane():
        pltpu.make_async_copy(pair_r, pair_r, rs_recv.at[0]).wait()
        first_half = iota((1, 1, 8, 128), 2) < 4
        tiles = score_s.shape[2]
        chips_y = dims["y"]

        def pair_step(zp, carry):
            even_at = pl.ds(2 * zp * chips_y, chips_y)
            odd_at = pl.ds((2 * zp + 1) * chips_y, chips_y)
            even = score_s[even_at, at["c"]] + pair_r[even_at]
            odd = score_s[odd_at, at["c"]] + pair_r[odd_at]
            even_turned, odd_turned = pltpu.roll(even, 4, 2), pltpu.roll(odd, 4, 2)
            lower = jnp.where(first_half, even, odd_turned)
            upper = jnp.where(first_half, even_turned, odd)
            for t in range(tiles):
                rs_a[:, 2 * t, zp] = lower[:, t]
                rs_a[:, 2 * t + 1, zp] = upper[:, t]
            return carry

        lax.fori_loop(0, dims["z"] // 2, pair_step, 0)
        rs_r1[plane_mine] = rs_a[at["y"], at["x"]]
        send_group(
            PLANE,
            lambda slot: rs_a.at[slot // dims["x"], slot % dims["x"]],
            rs_r1,
            rs_send.at[1],
            rs_recv.at[1],
        )

    def rivals_line():
        wait_group(rs_r1, rs_recv.at[1])
        rs_b[...] = tree_sum([rs_r1[k] for k in range(rs_r1.shape[0])])
        rs_r2[line_mine] = rs_b[at["z"] // 2]
        send_group(LINE, lambda slot: rs_b.at[slot // 2], rs_r2, rs_send.at[2], rs_recv.at[2])

    columns_total = float(pattern.shape[1] * dims["z"] * dims["y"] * dims["c"] * dims["x"])

    def rivals_finish():
        wait_group(rs_r2, rs_recv.at[2])
        total = tree_sum([rs_r2[k] for k in range(rs_r2.shape[0])]) / columns_total
        total = jnp.where(at["z"] % 2 == 0, total, pltpu.roll(total, 4, 0))
        out_scores[...] = pltpu.roll(total, 1, 1)[0:4, 0:CAND]

    pl.semaphore_wait(barrier, len(greeted))
    length = jnp.full((1, 128), root_length[0, 0], f32)

    def nothing():
        return None

    hidden = [(rivals_scores, rivals_plane), (rivals_line, rivals_finish), (nothing, nothing)]
    left_half = lane1 < 64
    for step in range(NEWTON):
        first, second = local_sums(length)
        folded = jnp.where(left_half, first + pltpu.roll(first, 64, 1), second + pltpu.roll(second, 64, 1))
        sums = all_sum(step, folded, *hidden[step])
        first = jnp.sum(jnp.where(left_half, sums, 0.0), axis=1, keepdims=True)
        second = jnp.sum(jnp.where(left_half, 0.0, sums), axis=1, keepdims=True)
        proposal = length - first / jnp.minimum(second, -1.0)
        length = jnp.clip(proposal, 0.25 * length, LENGTH_CAP)

    root_a[...] = length
    head_column = (at["z"] == 0) & (at["c"] == 0)
    head_plane = (at["y"] == 0) & (at["x"] == 0)

    @pl.when(head_column)
    def _():
        root_m[...] = length
        for _, dz, flip in column_offsets[1:]:
            send(root_a, root_b, root_send.at[0], root_recv.at[0], peer_at(dz, flip)[1])


    (value,) = series(length, (basis0,))
    loglik = jnp.log(value) + root_scale
    out_loglik[...] = loglik
    high = split_high(loglik)
    middle = split_high(loglik - high)
    low = loglik - high - middle
    row16 = iota((16, 128), 0)
    parts = pick(row16, [high, middle, low], jnp.zeros((16, 128), f32)).astype(bf16)
    gathered = jnp.dot(parts, onehot_b[...], preferred_element_type=f32).astype(bf16)
    own = lax.dot_general(gathered, w_b[...], (((1,), (1,)), ((), ())), preferred_element_type=f32)
    own = jnp.sum(own, axis=0, keepdims=True)
    if lanes_z != 128:
        row_v[...] = jnp.zeros_like(row_v)
    for z in range(dims["z"]):
        row_v[z, :, 0:lanes_z] = own[:, z * lanes_z : (z + 1) * lanes_z]
    for slot, (far, dz, flip) in reversed(list(enumerate(column_offsets))[1:]):
        there, device = peer_at(dz, flip)
        level = level_of(far, plane_needs)
        send(row_v.at[there["z"]], row_r1.at[slot], row_send.at[0], row_recv.at[level], device)
    for slot, offset in enumerate(direct_offsets):
        there, device = peer_at(*offset)
        send(row_v.at[there["z"]], row_d.at[slot], row_send.at[1], row_recv.at[LEVELS], device)

    def forward_row(level, distances, total):
        row_u[level] = total
        for slot, (wide, dy, dx) in reversed(list(enumerate(plane_offsets))[1:]):
            if wide in distances:
                device = peer_at(dy=dy, dx=dx)[1]
                send(row_u.at[level], row_r2.at[slot], row_send.at[2], row_recv.at[LEVELS + 1], device)

    total = relay(column_offsets, row_r1, row_recv, row_v[at["z"]], plane_needs, forward_row)

    @pl.when(jnp.logical_not(head_column))
    def _():
        wait_for(root_b, root_recv.at[0])
        root_m[...] = root_b[...]

    @pl.when(head_plane)
    def _():
        for _, dy, dx in plane_offsets[1:]:
            send(root_m, root_c, root_send.at[1], root_recv.at[1], peer_at(dy=dy, dx=dx)[1])

    wait_for(row_d, row_recv.at[LEVELS])
    total = total + tree_sum([row_d[k] for k in range(len(direct_offsets))])
    others = len(plane_offsets) - 1
    wait_for(row_r2.at[pl.ds(1, others)], row_recv.at[LEVELS + 1])
    total = total + tree_sum([row_r2[k] for k in range(1, others + 1)])
    total = total / columns_total
    shift = ((at["y"] * dims["c"] + at["c"]) * dims["x"] + at["x"]) * 4
    total = pltpu.roll(jnp.broadcast_to(total, (8, 128)), 128 - shift, 1)
    total = jnp.where(iota((8, 128), 0) == iota((8, 128), 1), total, 0.0)
    out_scores[:, 0:1] = jnp.sum(total, axis=1, keepdims=True)[0:4]

    @pl.when(jnp.logical_not(head_plane))
    def _():
        wait_for(root_c, root_recv.at[1])
        out_root[...] = root_c[...]

    @pl.when(head_plane)
    def _():
        out_root[...] = root_m[...]

    planes, columns = len(plane_offsets) - 1, len(column_offsets) - 1
    for step in range(NEWTON):
        wait_for(ar_a.at[step, pl.ds(1, planes)], ar_send.at[step, 0])
        wait_for(ar_d.at[step], ar_send.at[step, 1])
        wait_for(ar_b.at[step, pl.ds(1, columns)], ar_send.at[step, 2])
    wait_for(pair_r, rs_send.at[0])
    wait_group(rs_r1, rs_send.at[1])
    wait_group(rs_r2, rs_send.at[2])
    wait_for(row_r1.at[pl.ds(1, columns)], row_send.at[0])
    wait_for(row_d, row_send.at[1])
    wait_for(row_r2.at[pl.ds(1, planes)], row_send.at[2])

    @pl.when(head_column)
    def _():
        wait_for(row_r1.at[pl.ds(1, columns)], root_send.at[0])

    @pl.when(head_plane)
    def _():
        wait_for(row_r2.at[pl.ds(1, planes)], root_send.at[1])


def on_device(
    dims,
    taxa_states,
    outside,
    children,
    branch,
    root_length,
    cat_rates,
    exchange_rates,
    frequencies,
    rivals,
    pattern_idx,
    weights,
):
    reps, columns = weights.shape
    patterns = taxa_states.shape[1]
    z, y, c, x = (dims[a] for a in ("z", "y", "c", "x"))
    tiles = x // 2
    plane, column = group_size(dims, PLANE), group_size(dims, COLUMN)
    direct = len(routes(dims)[2])
    vmem = pl.BlockSpec(memory_space=pltpu.VMEM)
    hbm = pl.BlockSpec(memory_space=pl.ANY)
    scores, loglik, root = pl.pallas_call(
        functools.partial(kernel, dims),
        out_shape=(
            jax.ShapeDtypeStruct((4, CAND), f32),
            jax.ShapeDtypeStruct((1, patterns), f32),
            jax.ShapeDtypeStruct((1, 128), f32),
        ),
        in_specs=[hbm] * 11,
        out_specs=(vmem, vmem, vmem),
        scratch_shapes=[
            pltpu.VMEM(taxa_states.shape, jnp.int32),
            pltpu.VMEM((STATES, CATS, patterns), f32),
            pltpu.SMEM((2, INNER), jnp.int32),
            pltpu.SMEM(branch.shape, f32),
            pltpu.SMEM((1, 1), f32),
            pltpu.SMEM(cat_rates.shape, f32),
            pltpu.VMEM(exchange_rates.shape, f32),
            pltpu.SMEM(frequencies.shape, f32),
            pltpu.VMEM((1, columns), jnp.int32),
            pltpu.VMEM((reps, columns), jnp.int32),
            pltpu.VMEM((RIVALS, 128), f32),
            pltpu.VMEM((reps, columns), bf16),
            pltpu.VMEM((128, columns), bf16),
            pltpu.VMEM((128, 128), f32),
            pltpu.VMEM((TERMS * PAD, 128), f32),
            pltpu.VMEM((256, 128), f32),
            pltpu.VMEM((128 * STATES, 128), f32),
            pltpu.VMEM((128 * STATES, 128), f32),
            pltpu.VMEM((128 * STATES, 128), f32),
            pltpu.VMEM((EDGES, BLOCK, 128), f32),
            pltpu.VMEM((32, 128), f32),
            pltpu.VMEM((BLOCK, 128), f32),
            pltpu.VMEM((128, CATS * 128), f32),
            pltpu.VMEM((STATES * TERMS, 128), f32),
            pltpu.VMEM((STATES, CATS, 128), f32),
            pltpu.VMEM((CATS, TERMS + 8, 128), f32),
            pltpu.VMEM((z * y, c, tiles, 8, 128), f32),
            pltpu.VMEM((z * y, tiles, 8, 128), f32),
            pltpu.VMEM((y, x, z // 2, 8, 128), f32),
            pltpu.VMEM((plane, z // 2, 8, 128), f32),
            pltpu.VMEM((z // 2, 8, 128), f32),
            pltpu.VMEM((z, 8, 128), f32),
            pltpu.VMEM((NEWTON, 1, 128), f32),
            pltpu.VMEM((NEWTON, LEVELS, 1, 128), f32),
            pltpu.VMEM((NEWTON, plane, 1, 128), f32),
            pltpu.VMEM((NEWTON, column, 1, 128), f32),
            pltpu.VMEM((NEWTON, direct, 1, 128), f32),
            pltpu.VMEM((z, 1, 128), f32),
            pltpu.VMEM((column, 1, 128), f32),
            pltpu.VMEM((LEVELS, 1, 128), f32),
            pltpu.VMEM((plane, 1, 128), f32),
            pltpu.VMEM((direct, 1, 128), f32),
            pltpu.VMEM((1, 128), f32),
            pltpu.VMEM((1, 128), f32),
            pltpu.VMEM((1, 128), f32),
            pltpu.VMEM((1, 128), f32),
            pltpu.SemaphoreType.DMA((11,)),
            pltpu.SemaphoreType.DMA((NEWTON, 3)),
            pltpu.SemaphoreType.DMA((NEWTON, LEVELS + 2)),
            pltpu.SemaphoreType.DMA((3,)),
            pltpu.SemaphoreType.DMA((3,)),
            pltpu.SemaphoreType.DMA((3,)),
            pltpu.SemaphoreType.DMA((LEVELS + 2,)),
            pltpu.SemaphoreType.DMA((2,)),
            pltpu.SemaphoreType.DMA((2,)),
        ],
        compiler_params=pltpu.CompilerParams(
            collective_id=0, has_side_effects=True, vmem_limit_bytes=63 * 1024 * 1024
        ),
    )(
        taxa_states,
        outside.transpose(1, 0, 2),
        children.T,
        branch,
        root_length.reshape(1, 1),
        cat_rates,
        exchange_rates,
        frequencies,
        pattern_idx.reshape(1, columns),
        rivals,
        weights,
    )
    return scores.T, loglik.reshape(patterns), root[0, 0:1]


def solution(mesh):
    placed = (
        P(None, ("cols", "rep")),
        P(None, None, ("cols", "rep")),
        P(),
        P(),
        P(),
        P(),
        P(),
        P(),
        P(None, ("cols", "rep")),
        P(("cols", "rep")),
        P(None, ("cols", "rep")),
    )
    return jax.shard_map(
        functools.partial(on_device, layout_of(mesh)),
        mesh=mesh,
        in_specs=placed,
        out_specs=(P(None, ("cols", "rep")), P(("cols", "rep")), P()),
        check_vma=False,
    )
```

time: 84.1 us -> 72.6 us (0.86)
  local copies, waits for them, and re-layouts: 10.6 us -> 2.39 us
  Pallas kernels: 70.6 us -> 66.9 us
    unnamed x22 -> x2, local copies, waits for them, and re-layouts: 9.84 us -> 2.39 us
    pallas_call x1, Pallas kernels: 70.6 us -> 66.9 us  [on_device(): pl.pallas_call(functools.partial(kernel, dims), out_shape=(jax.ShapeDtype...]
where the time goes in v2:
time: 72.6 us; the launch traced here: 72.4 us
  Pallas kernels  66.9 us (92%)
  between operations  3.05 us (4%)
  local copies, waits for them, and re-layouts  2.39 us (3%)
    pallas_call x1, Pallas kernels, on_device(): pl.pallas_call(functools.partial(kernel, dims), out_shape=(jax.ShapeDtype...  66.9 us
    unnamed x2, local copies, waits for them, and re-layouts  2.39 us

profile of v2, /device:TPU:1, one launch (start us, length us, event | category | flops | bytes accessed | tf_op | source)
XLA Modules:
  0.0 72.4 jit_solution(6613786644697339685)
XLA Ops:
  1.3 66.9 %shard_map.130 = (f32[4,100]{1,0:T(4,128)}, f32[1,128]{1,0:T(1,128)}, f32[1,128]{1,0:T(1,128)}) custom-call(s32[32,128]{1,0:T(8,128)} %taxa_hbm.1, f32[20,4,128]{2,1,0:T(4,128)} %bitcast.9, s32[2,31]{1,0:T(2,128)} %bitcast.11, f32[62]{0:T(128)} %branch_hbm.1, f32[1,1]{1,0:T(1,128)} %bitcast.8.root_length_hbm, f32[4]{0:T(128)} %rates_hbm.1, ...), custom_call_target="tpu_custom_call" | custom-call | tf_op jit(solution)/shard_map/pallas_call | solution.py:694
  68.2 1.2 %copy.18 = f32[100,4]{0,1:T(4,128)} copy(f32[100,4]{0,1:T(4,128)} %bitcast.10) | data formatting | bytes 3200
  69.5 1.1 %copy.19 = f32[128]{0:T(128)} copy(f32[128]{0:T(128)} %bitcast.14) | data formatting | bytes 1024

commit v3 on v2

--- a/solution.py
+++ b/solution.py
@@ -99,12 +99,12 @@
     return min(step, size - step)
 
 
-def routes(dims):
+def routes(dims, slack):
     plane = sorted(
         ((ring(dy, dims["y"]) + ring(dx, dims["x"]), dy, dx) for dy in range(dims["y"]) for dx in range(dims["x"]))
     )
     column = sorted(((ring(dz, dims["z"]), dz, flip) for dz in range(dims["z"]) for flip in range(dims["c"])))
-    most = plane[-1][0] + column[-1][0] - DIRECT_SLACK
+    most = plane[-1][0] + column[-1][0] - slack
     direct = [
         (dz, flip, dy, dx)
         for far, dz, flip in reversed(column)
@@ -221,7 +221,8 @@
         loads[name] = pltpu.make_async_copy(source, target, load_sem.at[number])
         loads[name].start()
 
-    plane_offsets, column_offsets, direct_offsets, column_needs, plane_needs = routes(dims)
+    plane_offsets, column_offsets, direct_offsets, column_needs, plane_needs = routes(dims, DIRECT_SLACK)
+    no_direct = routes(dims, 0)
 
     def peer_at(dz=0, flip=0, dy=0, dx=0):
         core = at["c"] if flip == 0 else 1 - at["c"]
@@ -229,9 +230,8 @@
         return there, device_of(dims, there)
 
     barrier = pltpu.get_barrier_semaphore()
-    greeted = [peer_at(dz, flip)[1] for _, dz, flip in column_offsets[1:]]
-    greeted += [peer_at(dy=dy, dx=dx)[1] for _, dy, dx in plane_offsets[1:]]
-    greeted += [peer_at(*offset)[1] for offset in direct_offsets]
+    greeted = [peer_at(dz, flip)[1] for _, dz, flip in reversed(column_offsets[1:])]
+    greeted += [peer_at(dy=dy, dx=dx)[1] for _, dy, dx in reversed(plane_offsets[1:])]
     for device in greeted:
         pl.semaphore_signal(barrier, inc=1, device_id=device, device_id_type=MESH)
 
@@ -455,12 +455,13 @@
         return min(level for level, reach in enumerate(sorted(set(needs.values()))) if distance <= reach)
 
     def all_sum(step, row, meanwhile, meanwhile_later):
+        direct, needs = (no_direct[2], no_direct[3]) if step == 0 else (direct_offsets, column_needs)
         sems_s, sems_r = ar_send.at[step], ar_recv.at[step]
         val_a[step] = row
         for slot, (wide, dy, dx) in reversed(list(enumerate(plane_offsets))[1:]):
-            level = level_of(wide, column_needs)
+            level = level_of(wide, needs)
             send(val_a.at[step], ar_a.at[step, slot], sems_s.at[0], sems_r.at[level], peer_at(dy=dy, dx=dx)[1])
-        for slot, offset in enumerate(direct_offsets):
+        for slot, offset in enumerate(direct):
             send(val_a.at[step], ar_d.at[step, slot], sems_s.at[1], sems_r.at[LEVELS], peer_at(*offset)[1])
         meanwhile()
 
@@ -476,10 +477,11 @@
                         peer_at(dz, flip)[1],
                     )
 
-        total = relay(plane_offsets, ar_a.at[step], sems_r, row, column_needs, forward)
+        total = relay(plane_offsets, ar_a.at[step], sems_r, row, needs, forward)
         meanwhile_later()
-        wait_for(ar_d.at[step], sems_r.at[LEVELS])
-        total = total + tree_sum([ar_d[step, k] for k in range(len(direct_offsets))])
+        if direct:
+            wait_for(ar_d.at[step], sems_r.at[LEVELS])
+            total = total + tree_sum([ar_d[step, k] for k in range(len(direct))])
         others = len(column_offsets) - 1
         wait_for(ar_b.at[step, pl.ds(1, others)], sems_r.at[LEVELS + 1])
         return total + tree_sum([ar_b[step, k] for k in range(1, others + 1)])
@@ -651,7 +653,8 @@
     planes, columns = len(plane_offsets) - 1, len(column_offsets) - 1
     for step in range(NEWTON):
         wait_for(ar_a.at[step, pl.ds(1, planes)], ar_send.at[step, 0])
-        wait_for(ar_d.at[step], ar_send.at[step, 1])
+        if step > 0:
+            wait_for(ar_d.at[step], ar_send.at[step, 1])
         wait_for(ar_b.at[step, pl.ds(1, columns)], ar_send.at[step, 2])
     wait_for(pair_r, rs_send.at[0])
     wait_group(rs_r1, rs_send.at[1])
@@ -667,6 +670,21 @@
     @pl.when(head_plane)
     def _():
         wait_for(row_r2.at[pl.ds(1, planes)], root_send.at[1])
+
+
+def in_hbm(value):
+    return pltpu.with_memory_space_constraint(value, pltpu.HBM)
+
+
+def hand_over(scores, loglik, root, out_scores, out_loglik, out_root, sems):
+    copies = [
+        pltpu.make_async_copy(source, target, sems.at[number])
+        for number, (source, target) in enumerate(((scores, out_scores), (loglik, out_loglik), (root, out_root)))
+    ]
+    for copy in copies:
+        copy.start()
+    for copy in copies:
+        copy.wait()
 
 
 def on_device(
@@ -688,7 +706,7 @@
     z, y, c, x = (dims[a] for a in ("z", "y", "c", "x"))
     tiles = x // 2
     plane, column = group_size(dims, PLANE), group_size(dims, COLUMN)
-    direct = len(routes(dims)[2])
+    direct = len(routes(dims, DIRECT_SLACK)[2])
     vmem = pl.BlockSpec(memory_space=pltpu.VMEM)
     hbm = pl.BlockSpec(memory_space=pl.ANY)
     scores, loglik, root = pl.pallas_call(
@@ -758,21 +776,33 @@
             pltpu.SemaphoreType.DMA((2,)),
         ],
         compiler_params=pltpu.CompilerParams(
-            collective_id=0, has_side_effects=True, vmem_limit_bytes=63 * 1024 * 1024
+            collective_id=0, has_side_effects=True, vmem_limit_bytes=40 * 1024 * 1024
         ),
     )(
-        taxa_states,
-        outside.transpose(1, 0, 2),
-        children.T,
-        branch,
+        in_hbm(taxa_states),
+        in_hbm(outside.transpose(1, 0, 2)),
+        in_hbm(children.T),
+        in_hbm(branch),
         root_length.reshape(1, 1),
-        cat_rates,
-        exchange_rates,
-        frequencies,
-        pattern_idx.reshape(1, columns),
-        rivals,
-        weights,
+        in_hbm(cat_rates),
+        in_hbm(exchange_rates),
+        in_hbm(frequencies),
+        in_hbm(pattern_idx.reshape(1, columns)),
+        in_hbm(rivals),
+        in_hbm(weights),
     )
+    scores, loglik, root = pl.pallas_call(
+        hand_over,
+        out_shape=(
+            jax.ShapeDtypeStruct((4, CAND), f32),
+            jax.ShapeDtypeStruct((1, patterns), f32),
+            jax.ShapeDtypeStruct((1, 128), f32),
+        ),
+        in_specs=[hbm] * 3,
+        out_specs=(pl.BlockSpec(memory_space=pltpu.HBM),) * 3,
+        scratch_shapes=[pltpu.SemaphoreType.DMA((3,))],
+        compiler_params=pltpu.CompilerParams(vmem_limit_bytes=16 * 1024 * 1024),
+    )(scores, loglik, root)
     return scores.T, loglik.reshape(patterns), root[0, 0:1]
 
 

time: 72.6 us -> 67.3 us (0.927)
  local copies, waits for them, and re-layouts: 2.39 us -> 0 us
  between operations: 3.05 us -> 1.29 us
  Pallas kernels: 66.9 us -> 65.8 us
    unnamed x2 -> x0, local copies, waits for them, and re-layouts: 2.39 us -> none
    pallas_call x1, Pallas kernels: 66.9 us -> 65.2 us  [on_device(): pl.pallas_call(functools.partial(kernel, dims), out_shape=(jax.ShapeDtype...]
where the time goes in v3:
time: 67.3 us; the launch traced here: 67.1 us
  Pallas kernels  65.8 us (98%)
  between operations  1.29 us (2%)
    pallas_call x1, Pallas kernels, on_device(): pl.pallas_call(functools.partial(kernel, dims), out_shape=(jax.ShapeDtype...  65.2 us

profile of v3, /device:TPU:1, one launch (start us, length us, event | category | flops | bytes accessed | tf_op | source)
XLA Modules:
  0.0 67.1 jit_solution(1801442856841871259)
XLA Ops:
  1.3 65.2 %shard_map.130 = (f32[4,100]{1,0:T(4,128)S(1)}, f32[1,128]{1,0:T(1,128)S(1)}, f32[1,128]{1,0:T(1,128)S(1)}) custom-call(s32[32,128]{1,0:T(8,128)} %taxa_hbm.1, f32[20,4,128]{2,1,0:T(4,128)} %bitcast.9, s32[2,31]{1,0:T(2,128)} %bitcast.10, f32[62]{0:T(128)} %branch_hbm.1, f32[1,1]{1,0:T(1,128)} %bitcast.8.root_length_hbm, f32[4]{0:T(128)} %rates_hbm.1, ...), custom_call_target="tpu_custom_call" | custom-call | tf_op jit(solution)/shard_map/pallas_call | solution.py:712
  66.5 0.6 shard_map.131

commit v4 on v3

--- a/solution.py
+++ b/solution.py
@@ -155,6 +155,7 @@
     riv,
     w_b,
     onehot_b,
+    tallies,
     square,
     powers,
     x_col,
@@ -563,10 +564,20 @@
     pl.semaphore_wait(barrier, len(greeted))
     length = jnp.full((1, 128), root_length[0, 0], f32)
 
+    def pattern_tallies():
+        chunk = min(256, reps)
+        for begin in range(0, reps, chunk):
+            made = lax.dot_general(
+                onehot_b[...], w_b[begin : begin + chunk, :], (((1,), (1,)), ((), ())), preferred_element_type=f32
+            )
+            high = made.astype(bf16)
+            tallies[0:128, begin : begin + chunk] = high
+            tallies[128:256, begin : begin + chunk] = (made - high.astype(f32)).astype(bf16)
+
     def nothing():
         return None
 
-    hidden = [(rivals_scores, rivals_plane), (rivals_line, rivals_finish), (nothing, nothing)]
+    hidden = [(rivals_scores, rivals_plane), (rivals_line, rivals_finish), (pattern_tallies, nothing)]
     left_half = lane1 < 64
     for step in range(NEWTON):
         first, second = local_sums(length)
@@ -584,7 +595,7 @@
     @pl.when(head_column)
     def _():
         root_m[...] = length
-        for _, dz, flip in column_offsets[1:]:
+        for _, dz, flip in reversed(column_offsets[1:]):
             send(root_a, root_b, root_send.at[0], root_recv.at[0], peer_at(dz, flip)[1])
 
 
@@ -596,9 +607,8 @@
     low = loglik - high - middle
     row16 = iota((16, 128), 0)
     parts = pick(row16, [high, middle, low], jnp.zeros((16, 128), f32)).astype(bf16)
-    gathered = jnp.dot(parts, onehot_b[...], preferred_element_type=f32).astype(bf16)
-    own = lax.dot_general(gathered, w_b[...], (((1,), (1,)), ((), ())), preferred_element_type=f32)
-    own = jnp.sum(own, axis=0, keepdims=True)
+    own = jnp.dot(jnp.concatenate([parts, parts], axis=1), tallies[...], preferred_element_type=f32)
+    own = jnp.sum(own[0:8], axis=0, keepdims=True)
     if lanes_z != 128:
         row_v[...] = jnp.zeros_like(row_v)
     for z in range(dims["z"]):
@@ -611,24 +621,27 @@
         there, device = peer_at(*offset)
         send(row_v.at[there["z"]], row_d.at[slot], row_send.at[1], row_recv.at[LEVELS], device)
 
+    def pass_root_on():
+        @pl.when(jnp.logical_not(head_column))
+        def _():
+            wait_for(root_b, root_recv.at[0])
+            root_m[...] = root_b[...]
+
+        @pl.when(head_plane)
+        def _():
+            for _, dy, dx in reversed(plane_offsets[1:]):
+                send(root_m, root_c, root_send.at[1], root_recv.at[1], peer_at(dy=dy, dx=dx)[1])
+
     def forward_row(level, distances, total):
         row_u[level] = total
         for slot, (wide, dy, dx) in reversed(list(enumerate(plane_offsets))[1:]):
             if wide in distances:
                 device = peer_at(dy=dy, dx=dx)[1]
                 send(row_u.at[level], row_r2.at[slot], row_send.at[2], row_recv.at[LEVELS + 1], device)
+        if level == 0:
+            pass_root_on()
 
     total = relay(column_offsets, row_r1, row_recv, row_v[at["z"]], plane_needs, forward_row)
-
-    @pl.when(jnp.logical_not(head_column))
-    def _():
-        wait_for(root_b, root_recv.at[0])
-        root_m[...] = root_b[...]
-
-    @pl.when(head_plane)
-    def _():
-        for _, dy, dx in plane_offsets[1:]:
-            send(root_m, root_c, root_send.at[1], root_recv.at[1], peer_at(dy=dy, dx=dx)[1])
 
     wait_for(row_d, row_recv.at[LEVELS])
     total = total + tree_sum([row_d[k] for k in range(len(direct_offsets))])
@@ -732,6 +745,7 @@
             pltpu.VMEM((RIVALS, 128), f32),
             pltpu.VMEM((reps, columns), bf16),
             pltpu.VMEM((128, columns), bf16),
+            pltpu.VMEM((256, reps), bf16),
             pltpu.VMEM((128, 128), f32),
             pltpu.VMEM((TERMS * PAD, 128), f32),
             pltpu.VMEM((256, 128), f32),

time: 67.3 us -> 67.1 us (level)
  no operation moved by 1% of the time
where the time goes in v4:
time: 67.1 us; the launch traced here: 66.9 us
  Pallas kernels  65.6 us (98%)
  between operations  1.29 us (2%)
    pallas_call x1, Pallas kernels, on_device(): pl.pallas_call(functools.partial(kernel, dims), out_shape=(jax.ShapeDtype...  65 us

profile of v4, /device:TPU:1, one launch (start us, length us, event | category | flops | bytes accessed | tf_op | source)
XLA Modules:
  0.0 66.9 jit_solution(107812847418433841)
XLA Ops:
  1.3 65.0 %shard_map.130 = (f32[4,100]{1,0:T(4,128)S(1)}, f32[1,128]{1,0:T(1,128)S(1)}, f32[1,128]{1,0:T(1,128)S(1)}) custom-call(s32[32,128]{1,0:T(8,128)} %taxa_hbm.1, f32[20,4,128]{2,1,0:T(4,128)} %bitcast.9, s32[2,31]{1,0:T(2,128)} %bitcast.10, f32[62]{0:T(128)} %branch_hbm.1, f32[1,1]{1,0:T(1,128)} %bitcast.8.root_length_hbm, f32[4]{0:T(128)} %rates_hbm.1, ...), custom_call_target="tpu_custom_call" | custom-call | tf_op jit(solution)/shard_map/pallas_call | solution.py:725
  66.3 0.6 shard_map.131
